TPU v7x, 256 devices: a whole 4x4x8 slice. The times are simulated.
256 devices in a mesh: rep: 8 (over y, core), grp: 32 (over x, z).
Axes of the slice: x: 4, y: 4, z: 8, core: 2. Of those that a mesh axis runs over, the one named last changes fastest.
Arguments:
- grad_parts: bfloat16 [8, 32, 256, 8192], P('rep', 'grp'), may hold values from -180 to 180
- stats: float32 [128, 2, 256, 256], P('grp'), may hold values from -0.2 to 34, as said below
- owner: int32 [32], replicated, may hold values from 0 to 31, as said below
Outputs:
- direction: float32 [256, 8192], P('grp')
- new_stats: float32 [128, 2, 256, 256], P('grp')
Inputs may be any that keep to these rules, and one draw needn't show every extreme that they name: `stats`: each left and right statistic is symmetric with a positive diagonal that exceeds the sum of magnitudes off the diagonal in its row. `owner`: no device owns more than 4 blocks, and some device owns exactly 4.
All inputs are finite; a program needn't handle non-finite values.
Results may differ from a plain program's by a relative error of at most 0.0003.
Values may be sent and summed in bfloat16 or wider, within the bound.
A program may use at most 128 MiB of HBM per device.

v0:
```python
import jax
import jax.numpy as jnp
from jax import lax
from jax.sharding import PartitionSpec as P

BS = 256
ITERS = 6


decay_rate = 0.9


def exact_dot(left_mat, right_mat):
    return jnp.matmul(left_mat, right_mat, precision=lax.Precision.HIGHEST)


def inverse_root(matrix):
    size = matrix.shape[-1]
    identity = jnp.eye(size, dtype=jnp.float32)
    norm_value = jnp.sqrt(jnp.sum(matrix * matrix, axis=(-2, -1), keepdims=True))
    result = identity * norm_value ** (-0.25)
    normalized = matrix / norm_value
    for iteration in range(ITERS):
        factor = (5.0 * identity - normalized) * 0.25
        result = exact_dot(result, factor)
        square = exact_dot(factor, factor)
        normalized = exact_dot(exact_dot(square, square), normalized)
    return result


def local(grad_parts, stats, owner):
    group_count = lax.axis_size("grp")
    replica_count = lax.axis_size("rep")
    row_count, col_count = (grad_parts.shape[2], grad_parts.shape[3])
    row_share = row_count // group_count
    partial_value = grad_parts[0, 0].astype(jnp.float32)
    group_shard = lax.psum_scatter(partial_value, "grp", scatter_dimension=0, tiled=True)
    flat_shard = lax.psum(group_shard, "rep")
    flat_shard = flat_shard / (group_count * replica_count)
    slot_count = stats.shape[0]
    blocks_row = col_count // BS
    block_total = owner.shape[0]
    group_index = lax.axis_index("grp")
    block_ids = jnp.arange(block_total, dtype=jnp.int32)
    same_owner = owner[:, None] == owner[None, :]
    earlier = block_ids[:, None] > block_ids[None, :]
    block_rank = jnp.sum((same_owner & earlier).astype(jnp.int32), axis=1)
    count_mine = jnp.sum((owner == group_index).astype(jnp.int32))
    target = owner * slot_count + block_rank
    slot_ids = jnp.arange(group_count * slot_count, dtype=jnp.int32)
    selector = (slot_ids[:, None] == target[None, :]).astype(jnp.float32)
    pieces = flat_shard.reshape(row_share, blocks_row, BS)
    outgoing = jnp.einsum("sj,rjc->src", selector, pieces, precision=lax.Precision.HIGHEST)
    outgoing = outgoing.reshape(group_count, slot_count, row_share, BS)
    incoming = lax.all_to_all(outgoing, "grp", split_axis=0, concat_axis=0, tiled=True)
    sub_count = BS // row_share
    owned_blocks = incoming.reshape(row_count // BS, sub_count, slot_count, row_share, BS).sum(0)
    owned_blocks = owned_blocks.transpose(1, 0, 2, 3).reshape(slot_count, BS, BS)
    left_stat = decay_rate * stats[:, 0] + exact_dot(
        owned_blocks, jnp.swapaxes(owned_blocks, -1, -2)
    )
    right_stat = decay_rate * stats[:, 1] + exact_dot(
        jnp.swapaxes(owned_blocks, -1, -2), owned_blocks
    )
    updated = jnp.stack([left_stat, right_stat], axis=1)
    live_slot = jnp.arange(slot_count) < count_mine
    new_stats = jnp.where(live_slot[:, None, None, None], updated, stats)

    def one_block(slot_index, root_pairs):
        stat_pair = lax.dynamic_index_in_dim(updated, slot_index, 0, keepdims=False)
        return lax.dynamic_update_index_in_dim(root_pairs, inverse_root(stat_pair), slot_index, 0)

    root_pairs = lax.fori_loop(0, count_mine, one_block, jnp.zeros_like(updated))
    precond = exact_dot(exact_dot(root_pairs[:, 0], owned_blocks), root_pairs[:, 1])
    grad_square, precond_square = lax.psum(
        (jnp.sum(owned_blocks * owned_blocks), jnp.sum(precond * precond)), "grp"
    )
    graft_ratio = jnp.sqrt(grad_square / precond_square)
    update_blocks = precond * graft_ratio
    slot_range = jnp.arange(slot_count, dtype=jnp.int32)
    slot_hit = (owner == group_index)[None, :] & (block_rank[None, :] == slot_range[:, None])
    row_range = jnp.arange(row_count // BS, dtype=jnp.int32)
    in_row = (block_ids // blocks_row)[None, :] == row_range[:, None]
    row_match = jnp.any(in_row[:, None, :] & slot_hit[None, :, :], axis=2)
    sub_pieces = update_blocks.reshape(slot_count, sub_count, row_share, BS).transpose(1, 0, 2, 3)
    outgoing_back = jnp.where(
        row_match[:, None, :, None, None], sub_pieces[None], jnp.zeros((), jnp.float32)
    )
    outgoing_back = outgoing_back.reshape(group_count, slot_count, row_share, BS)
    returned = lax.all_to_all(outgoing_back, "grp", split_axis=0, concat_axis=0, tiled=True)
    picker = (target[:, None] == slot_ids[None, :]).astype(jnp.float32)
    own_rows = jnp.einsum(
        "js,src->rjc",
        picker,
        returned.reshape(group_count * slot_count, row_share, BS),
        precision=lax.Precision.HIGHEST,
    )
    direction = own_rows.reshape(row_share, col_count)
    return (direction, new_stats)


def solution(mesh):
    return jax.shard_map(
        local,
        mesh=mesh,
        in_specs=(P("rep", "grp", None, None), P("grp", None, None, None), P()),
        out_specs=(P("grp", None), P("grp", None, None, None)),
        check_vma=False,
    )
```

profile of v0, /device:TPU:32, one launch (start us, length us, event | category | flops | bytes accessed | tf_op | source)
XLA Modules:
  0.0 528.0 jit_solution(753426105694786253)
XLA Ops:
  7.2 6.4 %bitcast_convert_fusion = f32[256,8192]{1,0:T(8,128)} fusion(bf16[1,1,256,8192]{3,2,1,0:T(8,128)(2,1)} %param.5), kind=kLoop, calls=%fused_computation.60 | loop fusion | flops 2097152 | bytes 12582912 | tf_op jit(solution)/shard_map/convert_element_type | solution.py:36
  14.4 229.6 %reduce-scatter.2.cloned.1.call-done = f32[8,8192]{1,0:T(8,128)} async-done(((f32[256,8192]{1,0:T(8,128)}), f32[8,8192]{1,0:T(8,128)}) %reduce-scatter.2.cloned.1.call-update) | async-done | bytes 262160 | tf_op jit(solution)/shard_map/reduce_scatter | solution.py:37
  244.7 66.0 %all-reduce.3.cloned.1.call-done = f32[8,8192]{1,0:T(8,128)} async-done(((f32[8,8192]{1,0:T(8,128)}), f32[8,8192]{1,0:T(8,128)}) %all-reduce.3.cloned.1.call-update) | async-done | bytes 262160 | tf_op jit(solution)/shard_map/psum | solution.py:38
  310.7 1.0 broadcast_multiply_fusion
  312.3 1.6 copy.35
  313.9 10.0 %all-to-all-start = ((f32[32,4,8,256]{3,2,1,0:T(8,128)}), f32[32,4,8,256]{3,2,1,0:T(8,128)S(1)}, u32[]{:S(2)}, u32[]{:S(2)}) async-start(f32[32,4,8,256]{3,2,1,0:T(8,128)} %copy.35), calls=%async_computation.1 | async-start | bytes 2097152 | tf_op jit(solution)/shard_map/all_to_all | solution.py:55
  324.8 25.8 %all-to-all-done = f32[32,4,8,256]{3,2,1,0:T(8,128)S(1)} async-done(((f32[32,4,8,256]{3,2,1,0:T(8,128)}), f32[32,4,8,256]{3,2,1,0:T(8,128)S(1)}, u32[]{:S(2)}, u32[]{:S(2)}) %all-to-all-start) | async-done | bytes 1048608 | tf_op jit(solution)/shard_map/all_to_all | solution.py:55
  350.6 1.9 fusion.49
  352.5 1.2 fusion.50
  354.1 1.8 broadcast_select_fusion
  355.9 1.5 broadcast_in_dim.22.clone
  357.4 17.5 %while.10 = (s32[]{:T(128)}, f32[4,2,256,256]{3,2,0,1:T(8,128)}, s32[]{:T(128)}, f32[4,2,256,256]{3,2,0,1:T(8,128)S(1)}, s32[]{:T(128)}, /*index=5*/s32[]{:T(128)}, s32[]{:T(128)}) while((s32[]{:T(128)}, f32[4,2,256,256]{3,2,0,1:T(8,128)}, s32[]{:T(128)}, f32[4,2,256,256]{3,2,0,1:T(8,128)S(1)}, s32[]{:T(128)}, /*index=5*/s32[]{:T(128)}, ...), condition=%wide.region_7.8_spmd, body=%wide.region_5.7_spmd.sunk | while | flops 8459649024 | bytes 31459500 | solution.py:73
  358.5 0.8 fusion.201
  359.3 0.8 fusion.202
  372.5 1.5 fusion.221
  374.8 2.5 fusion.56
  377.4 1.9 multiply_reduce_fusion
  379.3 0.9 fusion.61
  380.1 96.5 %all-reduce = (f32[]{:T(128)}, f32[]{:T(128)}) all-reduce(f32[]{:T(128)} %fusion.61, f32[]{:T(128)} %get-tuple-element.67), channel_id=1, replica_groups=mesh['rep'=8,'grp'=32] {'grp'}, use_global_device_ids=true, to_apply=%region_9.10 | all-reduce | flops 2 | bytes 16 | tf_op jit(solution)/shard_map/psum | solution.py:75
  478.0 1.2 fusion.62
  479.2 21.6 %all-to-all-start.1 = ((f32[32,4,8,256]{3,2,1,0:T(8,128)}), f32[32,4,8,256]{3,2,1,0:T(8,128)S(1)}, u32[]{:S(2)}, u32[]{:S(2)}) async-start(f32[32,4,8,256]{3,2,1,0:T(8,128)} %fusion.62), calls=%async_computation.2 | async-start | bytes 2097152 | tf_op jit(solution)/shard_map/all_to_all | solution.py:90
  500.9 1.5 copy.45
  502.4 17.2 %all-to-all-done.1 = f32[32,4,8,256]{3,2,1,0:T(8,128)S(1)} async-done(((f32[32,4,8,256]{3,2,1,0:T(8,128)}), f32[32,4,8,256]{3,2,1,0:T(8,128)S(1)}, u32[]{:S(2)}, u32[]{:S(2)}) %all-to-all-start.1) | async-done | bytes 1048608 | tf_op jit(solution)/shard_map/all_to_all | solution.py:90
  520.3 0.9 copy.55
  (44 shorter events, 16.6 us)
Async XLA Ops:
  7.2 236.9 %reduce-scatter.2.cloned.1.call-start = ((), (), s32[]{:S(2)}) async-start(), calls=%async_computation.3 | async-start | bytes 8650752 | tf_op jit(solution)/shard_map/reduce_scatter | solution.py:37
  13.6 0.7 copy-start.4
  13.6 297.1 %all-reduce.3.cloned.1.call-start = ((), (), s32[]{:S(2)}) async-start(), calls=%async_computation.4 | async-start | bytes 524288 | tf_op jit(solution)/shard_map/psum | solution.py:38
  312.3 38.3 %copy-start.1 = (f32[4,2,256,256]{3,2,1,0:T(8,128)S(1)}, f32[4,2,256,256]{3,2,1,0:T(8,128)}, u32[]{:S(2)}) copy-start(f32[4,2,256,256]{3,2,1,0:T(8,128)} %param.6) | copy-start | bytes 6291460
  313.9 36.7 %all-to-all-start = ((f32[32,4,8,256]{3,2,1,0:T(8,128)}), f32[32,4,8,256]{3,2,1,0:T(8,128)S(1)}, u32[]{:S(2)}, u32[]{:S(2)}) async-start(f32[32,4,8,256]{3,2,1,0:T(8,128)} %copy.35), calls=%async_computation.1 | async-start | bytes 2097152 | tf_op jit(solution)/shard_map/all_to_all | solution.py:55
  352.5 1.6 copy-start.2
  374.8 2.5 copy-start
  478.0 22.8 %copy-start.3 = (f32[4,2,256,256]{3,2,0,1:T(8,128)S(1)}, f32[4,2,256,256]{3,2,0,1:T(8,128)}, u32[]{:S(2)}) copy-start(f32[4,2,256,256]{3,2,0,1:T(8,128)} %get-tuple-element.64) | copy-start | bytes 6291460
  479.2 40.3 %all-to-all-start.1 = ((f32[32,4,8,256]{3,2,1,0:T(8,128)}), f32[32,4,8,256]{3,2,1,0:T(8,128)S(1)}, u32[]{:S(2)}, u32[]{:S(2)}) async-start(f32[32,4,8,256]{3,2,1,0:T(8,128)} %fusion.62), calls=%async_computation.2 | async-start | bytes 2097152 | tf_op jit(solution)/shard_map/all_to_all | solution.py:90
Sparse Core Ops, SparseCore 0:
  13.8 230.2 reduce-scatter.1
  246.5 64.2 all-reduce.2
where the time goes:
time: 528 us
  waiting for transfers between devices  339 us (64%)
  blocking collectives  96.5 us (18%)
  starting transfers between devices  31.7 us (6%)
  matrix products  24.1 us (5%)
  between operations  15.6 us (3%)
  other arithmetic  13 us (2%)
  local copies, waits for them, and re-layouts  6.5 us (1%)
    reduce_scatter x1, waiting for transfers between devices, local(): lax.psum_scatter(partial_value, 'grp', scatter_dimension=0, tiled=True)  230 us
    psum x1, blocking collectives, local(): lax.psum((jnp.sum(owned_blocks * owned_blocks), jnp.sum(precond * precond...  96.5 us
    psum x1, waiting for transfers between devices, local(): flat_shard = lax.psum(group_shard, 'rep')  66 us
    all_to_all x1, waiting for transfers between devices, local(): lax.all_to_all(outgoing, 'grp', split_axis=0, concat_axis=0, tiled=True)  25.8 us
    dot_general x25, matrix products, exact_dot(): return jnp.matmul(left_mat, right_mat, precision=lax.Precision.HIGHEST)  22.8 us
    all_to_all x1, starting transfers between devices, local(): lax.all_to_all(outgoing_back, 'grp', split_axis=0, concat_axis=0, tiled=T...  21.6 us
    all_to_all x1, waiting for transfers between devices, local(): lax.all_to_all(outgoing_back, 'grp', split_axis=0, concat_axis=0, tiled=T...  17.2 us
  transfers between devices with their start and end apart: 4, of which 4 were waited for; matrix products, arithmetic and copies ran while one was open for 1% of the time, Pallas kernels for 0%

commit v1 on v0

v1 whole, which is shorter than its diff:
```python
import functools
import jax
import jax.numpy as jnp
from jax import lax
from jax.experimental import pallas as pl
from jax.experimental.pallas import tpu as pltpu
from jax.sharding import PartitionSpec as P

BS = 256
ITERS = 6
DECAY = 0.9
NX, NY, NZ, NC = 4, 4, 8, 2
NB, SLOTS = 32, 4
MESH = pl.DeviceIdType.MESH
F32, BF16, I16 = jnp.float32, jnp.bfloat16, jnp.int16
TOP = 32700.0


def split(a):
    hi = a.astype(BF16)
    return hi, (a - hi.astype(F32)).astype(BF16)


def dot3(a, b):
    rows = a[0].shape[0]
    both = jnp.dot(jnp.concatenate(a, axis=0), b[0], preferred_element_type=F32)
    return both[:rows] + (both[rows:] + jnp.dot(a[0], b[1], preferred_element_type=F32))


def scale_of(code):
    return jnp.exp2(code * 0.125) * (1.0 / TOP)


def code_of(top):
    return jnp.ceil(jnp.log2(jnp.maximum(top, 1e-30)) * 8.0)


def rounded(v, inverse):
    q = (v * inverse + 12582912.0) - 12582912.0
    return to16(q.reshape(v.shape[0] * 8, 128))


def peak(v):
    return jnp.max(jnp.abs(v), axis=0)


def narrow(v):
    code = code_of(jnp.max(peak(v), axis=0, keepdims=True))
    return rounded(v, 1.0 / scale_of(code)), code


def to16(v):
    return v.astype(jnp.int32).astype(I16)


def wide(q):
    return q.astype(jnp.int32)


def sum_rows(v):
    v = jnp.maximum(v, 1e-36)
    e = jnp.floor(jnp.log2(v))
    return [e, jnp.round((v * jnp.exp2(-e) - 1.0) * 16000.0)]


def sums_from(rows):
    return jnp.exp2(rows[0:1]) * (1.0 + rows[1:2] * (1.0 / 16000.0))


def tail(rows):
    left = 16 - sum(r.shape[0] for r in rows)
    zero = [jnp.zeros((left, 128), F32)] if left else []
    return to16(jnp.concatenate(list(rows) + zero, axis=0))


def kernel(
    grad, stats_hbm, owner_hbm,
    fq, ratio_ref, ns,
    stats, own, sib,
    m1, rm1, red, m2, rm2, s_buf, m3, rm3, c3, rc3, gx0, gx1, gc0, gc1, m5, rm5, c5, rc5, gq, gbuf, codes, acc,
    xs, qs, xother, ma, rma, my, rmy,
    owner, rank, local_j,
    s_owner, s_own, s_stat, s_sib, r_sib, s_1, r_1, s_2, r_2, s_3, r_3, s_4, r_4, s_5, r_5,
    s_d, r_d, s_6, r_6, s_7, r_7, s_x, r_x, s_a, r_a, s_y, r_y, s_ag, r_ag,
):
    gx, gc = (gx0, gx1), (gc0, gc1)
    rep, grp = lax.axis_index("rep"), lax.axis_index("grp")
    y, c = lax.div(rep, 2), lax.rem(rep, 2)
    x, z = lax.div(grp, 8), lax.rem(grp, 8)

    def wrap(v, n):
        return lax.rem(v + n, n)

    def dev(dy=0, dc=0, dx=0, dz=0):
        return (wrap(y + dy, NY) * 2 + wrap(c + dc, 2), wrap(x + dx, NX) * 8 + wrap(z + dz, NZ))

    pending = []

    def remote(src, dst, ssem, rsem, to):
        return pltpu.make_async_remote_copy(
            src_ref=src, dst_ref=dst, send_sem=ssem, recv_sem=rsem, device_id=to, device_id_type=MESH
        )

    def send(src, dst, ssem, rsem, to):
        copy = remote(src, dst, ssem, rsem, to)
        copy.start()
        pending.append(copy)
        return copy

    def flush():
        for q in pending:
            q.wait_send()
        pending.clear()

    def xcols(k):
        return pl.ds(pl.multiple_of(wrap(x + k, NX) * 1024, 1024), 1024)

    def chunk(axis, k, h, core=None):
        lead = () if core is None else (core,)
        if axis == 0:
            yy = pl.ds(0, 4) if h is None else pl.ds(2 * h, 2)
            return (yy,) + lead + (slice(None), xcols(k))
        cols = pl.ds(4096, 4096) if h is None else pl.ds(4096 + 2048 * h, 2048)
        return (wrap(y + k, NY),) + lead + (slice(None), cols)

    pieces_in_order = [(axis, k, h) for k, h in ((2, 0), (2, 1), (1, None), (-1, None), (0, None)) for axis in range(2)]
    def own_copy(i, axis, k, h):
        return pltpu.make_async_copy(grad.at[chunk(axis, k, h, c)], own.at[chunk(axis, k, h)], s_own.at[i])

    for i, piece in enumerate(pieces_in_order):
        own_copy(i, *piece).start()
    owner_copy = pltpu.make_async_copy(owner_hbm, owner, s_owner)
    owner_copy.start()
    stat_copy = pltpu.make_async_copy(stats_hbm, stats, s_stat)
    stat_copy.start()

    partners = [dict(dc=1)]
    partners += [dict(dx=j) for j in (1, -1, 2)] + [dict(dy=i) for i in (1, -1, 2)]
    partners += [dict(dz=k) for k in range(1, NZ)]
    barrier = pltpu.get_barrier_semaphore()
    for p in partners:
        pl.semaphore_signal(barrier, inc=1, device_id=dev(**p), device_id_type=MESH)
    pl.semaphore_wait(barrier, len(partners))

    oc = wrap(c + 1, 2)
    def sib_copy(i, axis, k, h):
        return remote(grad.at[chunk(axis, k, h, oc)], sib.at[chunk(axis, k, h)], s_sib.at[i], r_sib.at[i], dev(dc=1))

    def begin(copies):
        for q in copies:
            q.start()
            pending.append(q)

    for i, piece in enumerate(pieces_in_order):
        begin([sib_copy(i, *piece)])

    def ready(i, axis, k, h):
        own_copy(i, axis, k, h).wait()
        sib_copy(i, axis, k, h).wait_recv()

    def tile(v):
        return v.reshape(4, 8, 128)

    def unit(axis, k, h, a, b):
        if axis == 0:
            row, at = 2 * h + a, wrap(x + k, NX) * 1024 + b * 128
        else:
            row, at = wrap(y + k, NY), 4096 + 2048 * h + (a * 8 + b) * 128
        at = pl.ds(pl.multiple_of(at, 128), 128)
        return own[row, :, at].astype(F32) + sib[row, :, at].astype(F32)

    def unit_rows(n):
        return pl.ds(n * 32 if isinstance(n, int) else pl.multiple_of(n * 32, 32), 32)

    def scale_tile(rows):
        return scale_of(wide(rows).astype(F32)[0:8])

    def scale_tile(rows):
        return scale_of(wide(rows).astype(F32)[0:8])

    def part(u, axis, k, h, adds, flow):
        scales = [scale_tile(rm1[u, axis, f, pl.ds(256, 16)]) for f in adds]
        zero = jnp.zeros((8, 128), F32)
        tops = [zero, zero]
        for a in range(2):
            for i in range(4):
                v = tile(unit(axis, k, h, a, 2 * i + u))
                for f, scale in zip(adds, scales):
                    v = v + tile(wide(rm1[u, axis, f, unit_rows(4 * a + i)]).astype(F32)) * scale
                if flow is None:
                    red[u, axis, 2 * h + a, i] = v
                else:
                    acc[a, i] = v
                tops[a] = jnp.maximum(tops[a], peak(v))
        if flow is not None:
            tops = [jnp.maximum(tops[0], tops[1])] * 2
        codes = [code_of(t) for t in tops]
        inverse = [1.0 / scale_of(code) for code in codes]
        for a in range(2):
            for i in range(4):
                if flow is None:
                    m2[u, axis, 2 * h + a, unit_rows(i)] = rounded(red[u, axis, 2 * h + a, i], inverse[a])
                else:
                    m1[u, axis, flow, unit_rows(4 * a + i)] = rounded(acc[a, i], inverse[a])
            if flow is None:
                m2[u, axis, 2 * h + a, pl.ds(128, 16)] = tail([codes[a]])
        if flow is not None:
            m1[u, axis, flow, pl.ds(256, 16)] = tail([codes[0]])

    def flow_copy(u, axis, f, hop):
        to = dev(dx=hop) if axis == 0 else dev(dy=hop)
        return remote(m1.at[u, axis, f], rm1.at[u, axis, f], s_1.at[u, axis, f], r_1.at[u, axis, f], to)

    def arrived(u, axis, f):
        flow_copy(u, axis, f, 1).wait_recv()

    def far(u):
        def body(h, carry):
            for axis in range(2):
                if u == 0:
                    ready(2 * h + axis, axis, 2, h)
                part(u, axis, 2, h, [], h)
                flow_copy(u, axis, h, 1 - 2 * h).start()
            return carry

        lax.fori_loop(0, 2, body, 0)

    def near(u):
        def body(h, carry):
            hop = 2 * h - 1
            for axis in range(2):
                if u == 0:
                    ready(6 - 2 * h + axis, axis, hop, None)
                part(u, axis, hop, h, [], 2 + h)
                flow_copy(u, axis, 2 + h, hop).start()
            return carry

        lax.fori_loop(0, 2, body, 0)

    def onward(u):
        def body(h, carry):
            hop = 1 - 2 * h
            for axis in range(2):
                arrived(u, axis, h)
                part(u, axis, hop, h, [h], 4 + h)
                flow_copy(u, axis, 4 + h, hop).start()
            return carry

        lax.fori_loop(0, 2, body, 0)
        for axis in range(2):
            for f in range(6):
                pending.append(flow_copy(u, axis, f, 1))

    def p2_copy(u, axis, to, at, frm):
        return remote(m2.at[u, axis, to], rm2.at[u, axis, frm], s_2.at[u, axis, to], r_2.at[u, axis, frm], at)

    def p2_send(u, axis, to):
        me = (y, x)[axis]
        at = dev(dy=to - y) if axis == 0 else dev(dx=to - x)

        @pl.when(me != to)
        def _():
            p2_copy(u, axis, to, at, me).start()

    def last(u):
        def body(h, carry):
            for axis in range(2):
                arrived(u, axis, 2 + h)
                arrived(u, axis, 4 + h)
                part(u, axis, 0, h, [2 + h, 4 + h], None)
                p2_send(u, axis, 2 * h)
                p2_send(u, axis, 2 * h + 1)
            return carry

        if u == 0:
            for axis in range(2):
                ready(8 + axis, axis, 0, None)
        lax.fori_loop(0, 2, body, 0)

    def p3_copies(u, to, at, frm):
        return (remote(c3.at[u, to], rc3.at[u, frm], s_3.at[u, 0, to], r_3.at[u, 0, frm], at),
                remote(m3.at[u, to], rm3.at[u, frm], s_3.at[u, 1, to], r_3.at[u, 1, frm], at))

    def column_code(v):
        return code_of(jnp.max(peak(v), axis=0, keepdims=True))

    def along_z(u):
        scales = {}
        for axis in range(2):
            me = (y, x)[axis]
            for k in range(1, 4):
                frm = wrap(me - k, 4)
                q = p2_copy(u, axis, wrap(me + k, 4), dev(dc=1), frm)
                pending.append(q)
                q.wait_recv()
                scales[axis, k] = scale_tile(rm2[u, axis, frm, pl.ds(128, 16)])

        def sum2(j, carry):
            for axis in range(2):
                me = (y, x)[axis]
                v = red[u, axis, me, j]
                for k in range(1, 4):
                    v = v + tile(wide(rm2[u, axis, wrap(me - k, 4), unit_rows(j)]).astype(F32)) * scales[axis, k]
                to = 4 * axis + j
                s_buf[u, to] = v
                code = column_code(v)
                c3[u, to] = code
                m3[u, to] = rounded(v, 1.0 / scale_of(code))

                @pl.when(z != to)
                def _():
                    for q in p3_copies(u, to, dev(dz=to - z), z):
                        q.start()

            return carry

        lax.fori_loop(0, 4, sum2, 0)

    def p4_copies(u, src, k):
        return (remote(gc[u].at[src], gc[u].at[src], s_4.at[u, 0, k - 1], r_4.at[u, 0, k - 1], dev(dz=k)),
                remote(gx[u].at[src], gx[u].at[src], s_4.at[u, 1, k - 1], r_4.at[u, 1, k - 1], dev(dz=k)))

    def gather_z(u):
        piece = s_buf[u, z]
        for k in range(1, NZ):
            for q in p3_copies(u, wrap(z + k, NZ), dev(dc=1), wrap(z - k, NZ)):
                pending.append(q)
                q.wait_recv()
        for k in range(1, NZ):
            frm = wrap(z - k, NZ)
            piece = piece + tile(wide(rm3[u, frm]).astype(F32)) * scale_of(rc3[u, frm])
        piece = piece * (1.0 / 256.0)
        code = column_code(piece)
        gc[u][z] = code
        gx[u][z] = rounded(piece, 1.0 / scale_of(code))
        for k in (4, 3, 5, 2, 6, 1, 7):
            begin(p4_copies(u, z, k))
        return piece

    def p5_copies(u, e):
        at = dev(dy=e // 4, dx=e % 4)
        return (remote(c5.at[u, e], rc5.at[u, e], s_5.at[u, 0, e], r_5.at[u, 0, e], at),
                remote(m5.at[u, e], rm5.at[u, e], s_5.at[u, 1, e], r_5.at[u, 1, e], at))

    def route(u):
        for k in range(1, NZ):
            for q in p4_copies(u, wrap(z - k, NZ), k):
                q.wait_recv()
        for i in (2, 1, 3, 0):
            for j in (2, 1, 3, 0):
                e = i * 4 + j
                which = local_j[wrap(x + j, NX) * SLOTS + wrap(y + i, NY)]
                take = jnp.maximum(which, 0)
                c5[u, e] = jnp.where(which >= 0, gc[u][take], jnp.zeros((1, 128), F32))
                m5[u, e] = jnp.where(which >= 0, wide(gx[u][take]), jnp.zeros((32, 128), jnp.int32)).astype(I16)
                if e:
                    begin(p5_copies(u, e))

    def half_copy(u, core):
        return remote(gq.at[y, core, u], gq.at[y, core, u], s_d.at[u], r_d.at[u], dev(dc=1))

    def open_half(slot, core, u):
        for i in range(NY):
            scale = scale_of(wide(gq[slot, core, u, i, pl.ds(32, 16)]).astype(F32)[0:1])
            v = tile(wide(gq[slot, core, u, i, pl.ds(0, 32)]).astype(F32)) * scale
            gbuf[i, core, :, pl.ds(u * 128, 128)] = v.reshape(32, 128)

    def collect(u):
        for i in range(NY):
            parts = [(m5[u, 0], c5[u, 0])] if i == 0 else []
            for j in range(NX):
                e = i * 4 + j
                if e:
                    for q in p5_copies(u, e):
                        q.wait_recv()
                    parts.append((rm5[u, e], rc5[u, e]))
            rows = [wide(v[0]) for v in parts]
            yi = wrap(y - i, NY)
            gq[y, c, u, yi, pl.ds(0, 32)] = ((rows[0] + rows[1]) + (rows[2] + rows[3])).astype(I16)
            code = (parts[0][1] + parts[1][1]) + (parts[2][1] + parts[3][1])
            gq[y, c, u, yi, pl.ds(32, 16)] = tail([code])
        begin([half_copy(u, c)])

    def rank_row(b, carry):
        ob = owner[b]
        total = jnp.int32(0)
        for e in range(NB):
            total = total + jnp.where((owner[e] == ob) & (e < b), 1, 0)
        rank[b] = total
        return carry

    def find(i, carry):
        target = lax.div(i, SLOTS) * NZ + z
        slot = lax.rem(i, SLOTS)
        found = jnp.int32(-1)
        for j in range(8):
            b = 4 * x + j if j < 4 else 16 + 4 * x + j - 4
            found = jnp.where((owner[b] == target) & (rank[b] == slot), j, found)
        local_j[i] = found
        return carry

    far(0)
    near(0)
    far(1)
    onward(0)
    near(1)
    onward(1)
    owner_copy.wait()
    lax.fori_loop(0, NB, rank_row, 0)
    last(0)
    last(1)
    along_z(0)
    along_z(1)
    lax.fori_loop(0, NX * SLOTS, find, 0)
    n_mine = jnp.int32(0)
    for b in range(NB):
        n_mine = n_mine + jnp.where(owner[b] == grp, 1, 0)
    pieces = [gather_z(u) for u in range(2)]
    route(0)
    route(1)
    collect(0)
    collect(1)
    g_square = jnp.sum(jnp.sum(pieces[0] * pieces[0] + pieces[1] * pieces[1], axis=0), axis=0, keepdims=True)

    def block_copies(slot, core, ssem, rsem, to):
        return [remote(gq.at[slot, core], gq.at[slot, core], ssem, rsem, to)]

    for k in (2, 1, 3):
        begin(block_copies(y, c, s_6.at[k - 1], r_6.at[k - 1], dev(dy=k)))
    stat_copy.wait()
    for u in range(2):
        open_half(y, c, u)
    for u in range(2):
        half_copy(u, oc).wait_recv()
        open_half(y, oc, u)

    def put_stats(slot, side, value):
        ns[slot, side] = jnp.where(n_mine > slot, value, stats[slot, side])

    def slot_stats(slot):
        for core in range(NC):
            for u in range(2):
                open_half(slot, core, u)
        g = gbuf[...].reshape(BS, BS)
        gp, gtp = split(g), split(g.T)
        put_stats(slot, 0, DECAY * stats[slot, 0] + dot3(gp, gtp))
        put_stats(slot, 1, DECAY * stats[slot, 1] + dot3(gtp, gp))

    g = gbuf[...].reshape(BS, BS)
    gt = g.T
    first, second = jnp.where(c == 0, g, gt), jnp.where(c == 0, gt, g)
    first_p, second_p = split(first), split(second)
    mat = DECAY * stats[y, c] + dot3(first_p, second_p)
    put_stats(y, c, mat)
    norm = jnp.sqrt(jnp.sum(jnp.sum(mat * mat, axis=0, keepdims=True), axis=1, keepdims=True))
    five = jnp.where(
        lax.broadcasted_iota(jnp.int32, (BS, BS), 0) == lax.broadcasted_iota(jnp.int32, (BS, BS), 1), 1.25, 0.0
    ).astype(F32)
    q0 = mat / norm
    factor = five - 0.25 * q0
    xs[...] = factor * lax.rsqrt(jnp.sqrt(norm))

    def advance(factor, q):
        fp = split(factor)
        square = split(dot3(fp, fp))
        return dot3(split(dot3(square, square)), split(q))

    qs[...] = advance(factor, q0)

    def newton(i, carry):
        q = qs[...]
        factor = five - 0.25 * q
        xs[...] = dot3(split(xs[...]), split(factor))
        qs[...] = advance(factor, q)
        return carry

    lax.fori_loop(0, ITERS - 3, newton, 0)
    q = qs[...]
    factor = five - 0.25 * q
    fp = split(factor)
    x5 = dot3(split(xs[...]), fp)
    square = split(dot3(fp, fp))
    fourth = dot3(square, square)
    xs[...] = 1.25 * x5 - 0.25 * dot3(split(fourth), split(dot3(split(q), split(x5))))

    root_copy = send(xs, xother, s_x, r_x, dev(dc=1))
    one_side = dot3(split(xs[...]), first_p)
    one_half = one_side.T[:, 128:]
    for k in (1, 2, 3):
        yk = wrap(y - k, NY)
        for q in block_copies(yk, c, s_6.at[k - 1], r_6.at[k - 1], dev(dy=k)):
            q.wait_recv()
        begin(block_copies(yk, c, s_7.at[k - 1], r_7.at[k - 1], dev(dc=1)))
    root_copy.wait_recv()
    other = xother[...]
    prec = dot3(
        split(jnp.where(c == 0, one_side, other)), split(jnp.where(c == 0, other[:, :128], one_half))
    ).reshape(32, 8, 128)
    p_square = jnp.sum(jnp.sum(prec * prec, axis=0), axis=0, keepdims=True)
    p_code = code_of(jnp.max(peak(prec), axis=0, keepdims=True))
    inverse = 1.0 / scale_of(p_code)
    end = jnp.concatenate([p_code] + sum_rows(g_square) + sum_rows(p_square) + [jnp.zeros((3, 128), F32)], axis=0)
    for i in range(NX * NZ):
        rows = (prec[i] * inverse + 12582912.0) - 12582912.0
        ma[i] = to16(jnp.concatenate([rows, end], axis=0))

    w = []
    for k in (4, 3, 5, 2, 6, 1, 7, 0):
        for j in (2, 1, 3, 0):
            if k or j:
                e = j * 8 + k
                w.append(send(ma.at[wrap(x + j, NX) * 8 + wrap(z + k, NZ)], rma.at[e], s_a.at[e], r_a.at[e], dev(dx=j, dz=k)))
    rma[0] = ma[grp]
    flush()
    put_stats(y, oc, DECAY * stats[y, oc] + dot3(second_p, first_p))

    def other_slot(k):
        yk = wrap(y - k, NY)
        for q in block_copies(yk, oc, s_7.at[k - 1], r_7.at[k - 1], dev(dc=1)):
            q.wait_recv()
        slot_stats(yk)

    def sums_of(end, at):
        return sums_from(end[at:at + 2]), sums_from(end[at + 2:at + 4])

    def add(pairs):
        while len(pairs) > 1:
            pairs = [(a[0] + b[0], a[1] + b[1]) for a, b in zip(pairs[::2], pairs[1::2])]
        return pairs[0]

    other_slot(1)
    for q in w:
        q.wait_recv()

    def pick(i, carry):
        pair = []
        for u in range(2):
            b = 2 * i + u
            o = owner[b]
            at = wrap(x - lax.div(o, NZ), NX) * 8 + wrap(z - lax.rem(o, NZ), NZ)
            pair.append(jnp.where(rank[b] == y, wide(rma[at]), jnp.zeros((16, 128), jnp.int32)))
            codes[pl.ds(lax.rem(b, 8), 1)] = pair[u][8:9].astype(F32)
        rows = jnp.concatenate([v[0:8] for v in pair], axis=0).astype(I16)
        my[lax.div(i, 4), pl.ds(pl.multiple_of(lax.rem(i, 4) * 16, 16), 16)] = rows
        return carry

    for yy in range(NY):
        lax.fori_loop(4 * yy, 4 * yy + 4, pick, 0)
        my[yy, pl.ds(64, 16)] = tail([codes[...]])
    w = []
    for k in (2, 1, 3):
        w.append(send(my.at[wrap(y + k, NY)], rmy.at[k], s_y.at[k], r_y.at[k], dev(dy=k)))
    g_sum, p_sum = add([sums_of(wide(rma[e]).astype(F32), 9) for e in range(NX * NZ)])
    flush()
    other_slot(2)
    for q in w:
        q.wait_recv()
    ends = [wide(v).astype(F32) for v in (my[y, pl.ds(64, 16)], rmy[1, pl.ds(64, 16)],
                                          rmy[2, pl.ds(64, 16)], rmy[3, pl.ds(64, 16)])]
    block_codes = (ends[0][0:8] + ends[1][0:8]) + (ends[2][0:8] + ends[3][0:8])
    fq[c, y, pl.ds(0, 64)] = (
        (wide(my[y, pl.ds(0, 64)]) + wide(rmy[1, pl.ds(0, 64)]))
        + (wide(rmy[2, pl.ds(0, 64)]) + wide(rmy[3, pl.ds(0, 64)]))
    ).astype(I16)
    fq[c, y, pl.ds(64, 16)] = tail([block_codes] + sum_rows(g_sum) + sum_rows(p_sum) + [jnp.zeros((4, 128), F32)])

    def ag_copy(core, yy, e, to):
        return remote(fq.at[core, yy], fq.at[core, yy], s_ag.at[e], r_ag.at[e], to)

    for k in (2, 1, 3, 0):
        for o in range(2):
            e = k * 2 + o
            if e:
                begin([ag_copy(c, y, e, dev(dy=k, dc=o))])
    other_slot(3)
    for k in range(NY):
        for o in range(2):
            e = k * 2 + o
            if e:
                ag_copy(wrap(c + o, 2), wrap(y - k, NY), e, dev(dy=k, dc=o)).wait_recv()
    g_sum, p_sum = add([sums_of(wide(fq[core, yy, pl.ds(64, 16)]).astype(F32), 8) for core in range(NC) for yy in range(NY)])
    ratio = jnp.sqrt(jnp.sum(g_sum, axis=1, keepdims=True) / jnp.sum(p_sum, axis=1, keepdims=True))
    ratio_ref[...] = jnp.broadcast_to(ratio, (1, 128))
    flush()


def hand_over(fq, ratio, ns_in, dir_out, ns_out, direction, sems):
    copies = []
    for i in range(SLOTS):
        for j in range(2):
            for half in range(2):
                at = (i, j, pl.ds(128 * half, 128))
                copies.append(pltpu.make_async_copy(ns_in.at[at], ns_out.at[at], sems.at[2 + len(copies)]))
    for q in copies:
        q.start()
    for half in range(2):
        for yy in (2 * half, 2 * half + 1):
            for h in range(NC):
                block_scales = scale_of(wide(fq[h, yy, pl.ds(64, 16)]).astype(F32)) * ratio[...]
                for i in range(8):
                    both = wide(fq[h, yy, pl.ds(16 * (i // 2), 16)]).astype(F32)
                    at = (yy * 8 + i) * 256 + h * 128
                    direction[:, pl.ds(at, 128)] = both[8 * (i % 2):8 * (i % 2) + 8] * block_scales[i:i + 1]
        at = (slice(None), pl.ds(4096 * half, 4096))
        copies.append(pltpu.make_async_copy(direction.at[at], dir_out.at[at], sems.at[half]))
        copies[-1].start()
    for q in copies:
        q.wait()


def local(grad_parts, stats, owner):
    grad = grad_parts.reshape(NY, NC, 32, 8192)
    vm, dma = pltpu.VMEM, pltpu.SemaphoreType.DMA
    t = (8, 128)
    scratch = [
        vm((SLOTS, 2, BS, BS), F32),
        vm((NY, 32, 8192), BF16), vm((NY, 32, 8192), BF16),
        vm((2, 2, 6, 272, 128), I16), vm((2, 2, 6, 272, 128), I16),
        vm((2, 2, 4, 4, 4) + t, F32),
        vm((2, 2, 4, 144, 128), I16), vm((2, 2, 4, 144, 128), I16),
        vm((2, 8, 4) + t, F32),
        vm((2, 8, 32, 128), I16), vm((2, 8, 32, 128), I16),
        vm((2, 8, 1, 128), F32), vm((2, 8, 1, 128), F32),
        vm((8, 32, 128), I16), vm((8, 32, 128), I16),
        vm((8, 1, 128), F32), vm((8, 1, 128), F32),
        vm((2, 16, 32, 128), I16), vm((2, 16, 32, 128), I16),
        vm((2, 16, 1, 128), F32), vm((2, 16, 1, 128), F32),
        vm((SLOTS, NC, 2, NY, 48, 128), I16),
        vm((NY, NC, 32, BS), F32),
        vm((8, 128), F32), vm((2, 4, 4) + t, F32),
        vm((BS, BS), F32), vm((BS, BS), F32), vm((BS, BS), F32),
        vm((32, 16, 128), I16), vm((32, 16, 128), I16),
        vm((NY, 80, 128), I16), vm((NY, 80, 128), I16),
        pltpu.SMEM((NB,), jnp.int32), pltpu.SMEM((NB,), jnp.int32), pltpu.SMEM((NX * SLOTS,), jnp.int32),
        dma, dma((10,)), dma, dma((10,)), dma((10,)), dma((2, 2, 6)), dma((2, 2, 6)),
        dma((2, 2, 4)), dma((2, 2, 4)), dma((2, 2, 8)), dma((2, 2, 8)), dma((2, 2, 7)), dma((2, 2, 7)),
        dma((2, 2, 16)), dma((2, 2, 16)),
        dma((2,)), dma((2,)), dma((3,)), dma((3,)), dma((3,)), dma((3,)), dma, dma,
        dma((32,)), dma((32,)), dma((4,)), dma((4,)), dma((8,)), dma((8,)),
    ]
    results = pl.pallas_call(
        kernel,
        out_shape=(pltpu.VMEM((NC, NY, 80, 128), I16), pltpu.VMEM((1, 128), F32), pltpu.VMEM((SLOTS, 2, BS, BS), F32)),
        in_specs=[
            pl.BlockSpec(memory_space=pltpu.HBM),
            pl.BlockSpec(memory_space=pltpu.HBM),
            pl.BlockSpec(memory_space=pltpu.HBM),
        ],
        out_specs=(pl.BlockSpec(memory_space=pltpu.VMEM),) * 3,
        scratch_shapes=scratch,
        compiler_params=pltpu.CompilerParams(
            collective_id=0, has_side_effects=True, vmem_limit_bytes=51 * 1024 * 1024
        ),
        cost_estimate=pl.CostEstimate(flops=4_000_000_000, bytes_accessed=9_000_000, transcendentals=0),
    )(*[pltpu.with_memory_space_constraint(v, pltpu.HBM) for v in (grad, stats, owner)])
    return pl.pallas_call(
        hand_over,
        out_shape=(
            jax.ShapeDtypeStruct((8, 8192), F32),
            jax.ShapeDtypeStruct((SLOTS, 2, BS, BS), F32),
        ),
        in_specs=[pl.BlockSpec(memory_space=pltpu.VMEM)] * 3,
        out_specs=(pl.BlockSpec(memory_space=pltpu.HBM), pl.BlockSpec(memory_space=pltpu.HBM)),
        scratch_shapes=[vm((8, 8192), F32), dma((2 + 4 * SLOTS,))],
    )(*[pltpu.with_memory_space_constraint(v, pltpu.VMEM) for v in results])


def solution(mesh):
    return jax.shard_map(
        local,
        mesh=mesh,
        in_specs=(P("rep", "grp", None, None), P("grp", None, None, None), P()),
        out_specs=(P("grp", None), P("grp", None, None, None)),
        check_vma=False,
    )
```

time: 528 us -> 71.5 us (0.14)
  the two profiles are of different devices: /device:TPU:32 before, /device:TPU:1 now
where the time goes in v1:
time: 71.5 us; the launch traced here: 71.4 us
  Pallas kernels  70.7 us (99%)
    pallas_call x1, Pallas kernels, local(): pl.pallas_call(kernel, out_shape=(pltpu.VMEM((NC, NY, 80, 128), I16), plt...  69.2 us
    pallas_call x1, Pallas kernels, local(): pl.pallas_call(hand_over, out_shape=(jax.ShapeDtypeStruct((8, 8192), F32)...  1.54 us

profile of v1, /device:TPU:1, one launch (start us, length us, event | category | flops | bytes accessed | tf_op | source)
XLA Modules:
  0.0 71.4 jit_solution(6027361359531403324)
XLA Ops:
  0.6 69.2 %shard_map.50 = (s16[2,4,80,128]{3,2,1,0:T(8,128)(2,1)S(1)}, f32[1,128]{1,0:T(1,128)S(1)}, f32[4,2,256,256]{3,2,1,0:T(8,128)S(1)}) custom-call(bf16[4,2,32,8192]{3,2,1,0:T(8,128)(2,1)} %bitcast.1, f32[4,2,256,256]{3,2,1,0:T(8,128)} %stats_hbm.1, s32[32]{0:T(128)} %owner_hbm.1), custom_call_target="tpu_custom_call" | custom-call | flops 4000000000 | bytes 9000000 | tf_op jit(solution)/shard_map/pallas_call | solution.py:641
  69.8 1.5 %shard_map.51 = (f32[8,8192]{1,0:T(8,128)}, f32[4,2,256,256]{3,2,1,0:T(8,128)}) custom-call(s16[2,4,80,128]{3,2,1,0:T(8,128)(2,1)S(1)} %get-tuple-element.5.fq, f32[1,128]{1,0:T(1,128)S(1)} %get-tuple-element.6.ratio, f32[4,2,256,256]{3,2,1,0:T(8,128)S(1)} %get-tuple-element.7.ns_in), custom_call_target="tpu_custom_call" | custom-call | tf_op jit(solution)/shard_map/pallas_call | solution.py:656

commit v2 on v1

--- a/solution.py
+++ b/solution.py
@@ -456,24 +456,22 @@
     five = jnp.where(
         lax.broadcasted_iota(jnp.int32, (BS, BS), 0) == lax.broadcasted_iota(jnp.int32, (BS, BS), 1), 1.25, 0.0
     ).astype(F32)
-    q0 = mat / norm
+    q0 = mat * (1.0 / norm)
     factor = five - 0.25 * q0
     xs[...] = factor * lax.rsqrt(jnp.sqrt(norm))
 
-    def advance(factor, q):
-        fp = split(factor)
-        square = split(dot3(fp, fp))
-        return dot3(split(dot3(square, square)), split(q))
-
-    qs[...] = advance(factor, q0)
-
     def newton(i, carry):
         q = qs[...]
-        factor = five - 0.25 * q
-        xs[...] = dot3(split(xs[...]), split(factor))
-        qs[...] = advance(factor, q)
+        fp = split(five - 0.25 * q)
+        square = split(dot3(fp, fp))
+        x_next = dot3(split(xs[...]), fp)
+        qs[...] = dot3(split(dot3(square, square)), split(q))
+        xs[...] = x_next
         return carry
 
+    fp = split(factor)
+    square = split(dot3(fp, fp))
+    qs[...] = dot3(split(dot3(square, square)), split(q0))
     lax.fori_loop(0, ITERS - 3, newton, 0)
     q = qs[...]
     factor = five - 0.25 * q
@@ -544,12 +542,13 @@
         my[lax.div(i, 4), pl.ds(pl.multiple_of(lax.rem(i, 4) * 16, 16), 16)] = rows
         return carry
 
-    for yy in range(NY):
+    w = []
+    for k in (2, 1, 3, 0):
+        yy = wrap(y + k, NY)
         lax.fori_loop(4 * yy, 4 * yy + 4, pick, 0)
         my[yy, pl.ds(64, 16)] = tail([codes[...]])
-    w = []
-    for k in (2, 1, 3):
-        w.append(send(my.at[wrap(y + k, NY)], rmy.at[k], s_y.at[k], r_y.at[k], dev(dy=k)))
+        if k:
+            w.append(send(my.at[yy], rmy.at[k], s_y.at[k], r_y.at[k], dev(dy=k)))
     g_sum, p_sum = add([sums_of(wide(rma[e]).astype(F32), 9) for e in range(NX * NZ)])
     flush()
     other_slot(2)

time: 71.5 us -> 71.2 us (level)
  no operation moved by 1% of the time
where the time goes in v2:
time: 71.2 us; the launch traced here: 71.1 us
  Pallas kernels  70.5 us (99%)
    pallas_call x1, Pallas kernels, local(): pl.pallas_call(kernel, out_shape=(pltpu.VMEM((NC, NY, 80, 128), I16), plt...  68.9 us
    pallas_call x1, Pallas kernels, local(): pl.pallas_call(hand_over, out_shape=(jax.ShapeDtypeStruct((8, 8192), F32)...  1.54 us

profile of v2, /device:TPU:1, one launch (start us, length us, event | category | flops | bytes accessed | tf_op | source)
XLA Modules:
  0.0 71.1 jit_solution(17268958944798303629)
XLA Ops:
  0.6 68.9 %shard_map.50 = (s16[2,4,80,128]{3,2,1,0:T(8,128)(2,1)S(1)}, f32[1,128]{1,0:T(1,128)S(1)}, f32[4,2,256,256]{3,2,1,0:T(8,128)S(1)}) custom-call(bf16[4,2,32,8192]{3,2,1,0:T(8,128)(2,1)} %bitcast.1, f32[4,2,256,256]{3,2,1,0:T(8,128)} %stats_hbm.1, s32[32]{0:T(128)} %owner_hbm.1), custom_call_target="tpu_custom_call" | custom-call | flops 4000000000 | bytes 9000000 | tf_op jit(solution)/shard_map/pallas_call | solution.py:640
  69.6 1.5 %shard_map.51 = (f32[8,8192]{1,0:T(8,128)}, f32[4,2,256,256]{3,2,1,0:T(8,128)}) custom-call(s16[2,4,80,128]{3,2,1,0:T(8,128)(2,1)S(1)} %get-tuple-element.5.fq, f32[1,128]{1,0:T(1,128)S(1)} %get-tuple-element.6.ratio, f32[4,2,256,256]{3,2,1,0:T(8,128)S(1)} %get-tuple-element.7.ns_in), custom_call_target="tpu_custom_call" | custom-call | tf_op jit(solution)/shard_map/pallas_call | solution.py:655

commit v3 on v2

--- a/solution.py
+++ b/solution.py
@@ -78,7 +78,7 @@
     fq, ratio_ref, ns,
     stats, own, sib,
     m1, rm1, red, m2, rm2, s_buf, m3, rm3, c3, rc3, gx0, gx1, gc0, gc1, m5, rm5, c5, rc5, gq, gbuf, codes, acc,
-    xs, qs, xother, ma, rma, my, rmy,
+    xs, qs, xother, pbuf, ma, rma, my, rmy,
     owner, rank, local_j,
     s_owner, s_own, s_stat, s_sib, r_sib, s_1, r_1, s_2, r_2, s_3, r_3, s_4, r_4, s_5, r_5,
     s_d, r_d, s_6, r_6, s_7, r_7, s_x, r_x, s_a, r_a, s_y, r_y, s_ag, r_ag,
@@ -127,6 +127,12 @@
     def own_copy(i, axis, k, h):
         return pltpu.make_async_copy(grad.at[chunk(axis, k, h, c)], own.at[chunk(axis, k, h)], s_own.at[i])
 
+    partners = [dict(dc=1)]
+    partners += [dict(dx=j) for j in (1, -1, 2)] + [dict(dy=i) for i in (1, -1, 2)]
+    partners += [dict(dz=k) for k in range(1, NZ)]
+    barrier = pltpu.get_barrier_semaphore()
+    for p in partners:
+        pl.semaphore_signal(barrier, inc=1, device_id=dev(**p), device_id_type=MESH)
     for i, piece in enumerate(pieces_in_order):
         own_copy(i, *piece).start()
     owner_copy = pltpu.make_async_copy(owner_hbm, owner, s_owner)
@@ -134,12 +140,6 @@
     stat_copy = pltpu.make_async_copy(stats_hbm, stats, s_stat)
     stat_copy.start()
 
-    partners = [dict(dc=1)]
-    partners += [dict(dx=j) for j in (1, -1, 2)] + [dict(dy=i) for i in (1, -1, 2)]
-    partners += [dict(dz=k) for k in range(1, NZ)]
-    barrier = pltpu.get_barrier_semaphore()
-    for p in partners:
-        pl.semaphore_signal(barrier, inc=1, device_id=dev(**p), device_id_type=MESH)
     pl.semaphore_wait(barrier, len(partners))
 
     oc = wrap(c + 1, 2)
@@ -404,9 +404,9 @@
     far(1)
     onward(0)
     near(1)
-    onward(1)
     owner_copy.wait()
     lax.fori_loop(0, NB, rank_row, 0)
+    onward(1)
     last(0)
     last(1)
     along_z(0)
@@ -498,16 +498,20 @@
     p_code = code_of(jnp.max(peak(prec), axis=0, keepdims=True))
     inverse = 1.0 / scale_of(p_code)
     end = jnp.concatenate([p_code] + sum_rows(g_square) + sum_rows(p_square) + [jnp.zeros((3, 128), F32)], axis=0)
-    for i in range(NX * NZ):
-        rows = (prec[i] * inverse + 12582912.0) - 12582912.0
-        ma[i] = to16(jnp.concatenate([rows, end], axis=0))
+    pbuf[...] = prec
+
+    def pack_row(g):
+        rows = (pbuf[g] * inverse + 12582912.0) - 12582912.0
+        ma[g] = to16(jnp.concatenate([rows, end], axis=0))
 
     w = []
     for k in (4, 3, 5, 2, 6, 1, 7, 0):
         for j in (2, 1, 3, 0):
-            if k or j:
-                e = j * 8 + k
-                w.append(send(ma.at[wrap(x + j, NX) * 8 + wrap(z + k, NZ)], rma.at[e], s_a.at[e], r_a.at[e], dev(dx=j, dz=k)))
+            e = j * 8 + k
+            to = wrap(x + j, NX) * 8 + wrap(z + k, NZ)
+            pack_row(to)
+            if e:
+                w.append(send(ma.at[to], rma.at[e], s_a.at[e], r_a.at[e], dev(dx=j, dz=k)))
     rma[0] = ma[grp]
     flush()
     put_stats(y, oc, DECAY * stats[y, oc] + dot3(second_p, first_p))
@@ -628,7 +632,7 @@
         vm((NY, NC, 32, BS), F32),
         vm((8, 128), F32), vm((2, 4, 4) + t, F32),
         vm((BS, BS), F32), vm((BS, BS), F32), vm((BS, BS), F32),
-        vm((32, 16, 128), I16), vm((32, 16, 128), I16),
+        vm((32,) + t, F32), vm((32, 16, 128), I16), vm((32, 16, 128), I16),
         vm((NY, 80, 128), I16), vm((NY, 80, 128), I16),
         pltpu.SMEM((NB,), jnp.int32), pltpu.SMEM((NB,), jnp.int32), pltpu.SMEM((NX * SLOTS,), jnp.int32),
         dma, dma((10,)), dma, dma((10,)), dma((10,)), dma((2, 2, 6)), dma((2, 2, 6)),

time: 71.2 us -> 71.7 us (level)
  no operation moved by 1% of the time
where the time goes in v3:
time: 71.7 us; the launch traced here: 71.6 us
  Pallas kernels  71 us (99%)
    pallas_call x1, Pallas kernels, local(): pl.pallas_call(kernel, out_shape=(pltpu.VMEM((NC, NY, 80, 128), I16), plt...  69.4 us
    pallas_call x1, Pallas kernels, local(): pl.pallas_call(hand_over, out_shape=(jax.ShapeDtypeStruct((8, 8192), F32)...  1.54 us

profile of v3, /device:TPU:1, one launch (start us, length us, event | category | flops | bytes accessed | tf_op | source)
XLA Modules:
  0.0 71.6 jit_solution(67253944088403942)
XLA Ops:
  0.6 69.4 %shard_map.50 = (s16[2,4,80,128]{3,2,1,0:T(8,128)(2,1)S(1)}, f32[1,128]{1,0:T(1,128)S(1)}, f32[4,2,256,256]{3,2,1,0:T(8,128)S(1)}) custom-call(bf16[4,2,32,8192]{3,2,1,0:T(8,128)(2,1)} %bitcast.1, f32[4,2,256,256]{3,2,1,0:T(8,128)} %stats_hbm.1, s32[32]{0:T(128)} %owner_hbm.1), custom_call_target="tpu_custom_call" | custom-call | flops 4000000000 | bytes 9000000 | tf_op jit(solution)/shard_map/pallas_call | solution.py:644
  70.1 1.5 %shard_map.51 = (f32[8,8192]{1,0:T(8,128)}, f32[4,2,256,256]{3,2,1,0:T(8,128)}) custom-call(s16[2,4,80,128]{3,2,1,0:T(8,128)(2,1)S(1)} %get-tuple-element.5.fq, f32[1,128]{1,0:T(1,128)S(1)} %get-tuple-element.6.ratio, f32[4,2,256,256]{3,2,1,0:T(8,128)S(1)} %get-tuple-element.7.ns_in), custom_call_target="tpu_custom_call" | custom-call | tf_op jit(solution)/shard_map/pallas_call | solution.py:659

commit v4 on v2

--- a/solution.py
+++ b/solution.py
@@ -127,6 +127,12 @@
     def own_copy(i, axis, k, h):
         return pltpu.make_async_copy(grad.at[chunk(axis, k, h, c)], own.at[chunk(axis, k, h)], s_own.at[i])
 
+    partners = [dict(dc=1)]
+    partners += [dict(dx=j) for j in (1, -1, 2)] + [dict(dy=i) for i in (1, -1, 2)]
+    partners += [dict(dz=k) for k in range(1, NZ)]
+    barrier = pltpu.get_barrier_semaphore()
+    for p in partners:
+        pl.semaphore_signal(barrier, inc=1, device_id=dev(**p), device_id_type=MESH)
     for i, piece in enumerate(pieces_in_order):
         own_copy(i, *piece).start()
     owner_copy = pltpu.make_async_copy(owner_hbm, owner, s_owner)
@@ -134,12 +140,6 @@
     stat_copy = pltpu.make_async_copy(stats_hbm, stats, s_stat)
     stat_copy.start()
 
-    partners = [dict(dc=1)]
-    partners += [dict(dx=j) for j in (1, -1, 2)] + [dict(dy=i) for i in (1, -1, 2)]
-    partners += [dict(dz=k) for k in range(1, NZ)]
-    barrier = pltpu.get_barrier_semaphore()
-    for p in partners:
-        pl.semaphore_signal(barrier, inc=1, device_id=dev(**p), device_id_type=MESH)
     pl.semaphore_wait(barrier, len(partners))
 
     oc = wrap(c + 1, 2)
@@ -404,9 +404,9 @@
     far(1)
     onward(0)
     near(1)
-    onward(1)
     owner_copy.wait()
     lax.fori_loop(0, NB, rank_row, 0)
+    onward(1)
     last(0)
     last(1)
     along_z(0)
@@ -527,6 +527,7 @@
         return pairs[0]
 
     other_slot(1)
+    other_slot(2)
     for q in w:
         q.wait_recv()
 
@@ -551,7 +552,6 @@
             w.append(send(my.at[yy], rmy.at[k], s_y.at[k], r_y.at[k], dev(dy=k)))
     g_sum, p_sum = add([sums_of(wide(rma[e]).astype(F32), 9) for e in range(NX * NZ)])
     flush()
-    other_slot(2)
     for q in w:
         q.wait_recv()
     ends = [wide(v).astype(F32) for v in (my[y, pl.ds(64, 16)], rmy[1, pl.ds(64, 16)],

time: 71.2 us -> 71.7 us (level)
  no operation moved by 1% of the time
where the time goes in v4:
time: 71.7 us; the launch traced here: 71.6 us
  Pallas kernels  71 us (99%)
    pallas_call x1, Pallas kernels, local(): pl.pallas_call(kernel, out_shape=(pltpu.VMEM((NC, NY, 80, 128), I16), plt...  69.5 us
    pallas_call x1, Pallas kernels, local(): pl.pallas_call(hand_over, out_shape=(jax.ShapeDtypeStruct((8, 8192), F32)...  1.54 us

profile of v4, /device:TPU:1, one launch (start us, length us, event | category | flops | bytes accessed | tf_op | source)
XLA Modules:
  0.0 71.6 jit_solution(1166796199441929679)
XLA Ops:
  0.6 69.5 %shard_map.50 = (s16[2,4,80,128]{3,2,1,0:T(8,128)(2,1)S(1)}, f32[1,128]{1,0:T(1,128)S(1)}, f32[4,2,256,256]{3,2,1,0:T(8,128)S(1)}) custom-call(bf16[4,2,32,8192]{3,2,1,0:T(8,128)(2,1)} %bitcast.1, f32[4,2,256,256]{3,2,1,0:T(8,128)} %stats_hbm.1, s32[32]{0:T(128)} %owner_hbm.1), custom_call_target="tpu_custom_call" | custom-call | flops 4000000000 | bytes 9000000 | tf_op jit(solution)/shard_map/pallas_call | solution.py:640
  70.1 1.5 %shard_map.51 = (f32[8,8192]{1,0:T(8,128)}, f32[4,2,256,256]{3,2,1,0:T(8,128)}) custom-call(s16[2,4,80,128]{3,2,1,0:T(8,128)(2,1)S(1)} %get-tuple-element.5.fq, f32[1,128]{1,0:T(1,128)S(1)} %get-tuple-element.6.ratio, f32[4,2,256,256]{3,2,1,0:T(8,128)S(1)} %get-tuple-element.7.ns_in), custom_call_target="tpu_custom_call" | custom-call | tf_op jit(solution)/shard_map/pallas_call | solution.py:655

commit v5 on v4

--- a/solution.py
+++ b/solution.py
@@ -404,13 +404,13 @@
     far(1)
     onward(0)
     near(1)
-    owner_copy.wait()
-    lax.fori_loop(0, NB, rank_row, 0)
     onward(1)
     last(0)
     last(1)
     along_z(0)
     along_z(1)
+    owner_copy.wait()
+    lax.fori_loop(0, NB, rank_row, 0)
     lax.fori_loop(0, NX * SLOTS, find, 0)
     n_mine = jnp.int32(0)
     for b in range(NB):
@@ -527,7 +527,6 @@
         return pairs[0]
 
     other_slot(1)
-    other_slot(2)
     for q in w:
         q.wait_recv()
 
@@ -552,6 +551,7 @@
             w.append(send(my.at[yy], rmy.at[k], s_y.at[k], r_y.at[k], dev(dy=k)))
     g_sum, p_sum = add([sums_of(wide(rma[e]).astype(F32), 9) for e in range(NX * NZ)])
     flush()
+    other_slot(2)
     for q in w:
         q.wait_recv()
     ends = [wide(v).astype(F32) for v in (my[y, pl.ds(64, 16)], rmy[1, pl.ds(64, 16)],

time: 71.7 us -> 71.8 us (level)
  no operation moved by 1% of the time
where the time goes in v5:
time: 71.8 us; the launch traced here: 71.7 us
  Pallas kernels  71.1 us (99%)
    pallas_call x1, Pallas kernels, local(): pl.pallas_call(kernel, out_shape=(pltpu.VMEM((NC, NY, 80, 128), I16), plt...  69.5 us
    pallas_call x1, Pallas kernels, local(): pl.pallas_call(hand_over, out_shape=(jax.ShapeDtypeStruct((8, 8192), F32)...  1.54 us

profile of v5, /device:TPU:1, one launch (start us, length us, event | category | flops | bytes accessed | tf_op | source)
XLA Modules:
  0.0 71.7 jit_solution(3764793182957141505)
XLA Ops:
  0.6 69.5 %shard_map.50 = (s16[2,4,80,128]{3,2,1,0:T(8,128)(2,1)S(1)}, f32[1,128]{1,0:T(1,128)S(1)}, f32[4,2,256,256]{3,2,1,0:T(8,128)S(1)}) custom-call(bf16[4,2,32,8192]{3,2,1,0:T(8,128)(2,1)} %bitcast.1, f32[4,2,256,256]{3,2,1,0:T(8,128)} %stats_hbm.1, s32[32]{0:T(128)} %owner_hbm.1), custom_call_target="tpu_custom_call" | custom-call | flops 4000000000 | bytes 9000000 | tf_op jit(solution)/shard_map/pallas_call | solution.py:640
  70.2 1.5 %shard_map.51 = (f32[8,8192]{1,0:T(8,128)}, f32[4,2,256,256]{3,2,1,0:T(8,128)}) custom-call(s16[2,4,80,128]{3,2,1,0:T(8,128)(2,1)S(1)} %get-tuple-element.5.fq, f32[1,128]{1,0:T(1,128)S(1)} %get-tuple-element.6.ratio, f32[4,2,256,256]{3,2,1,0:T(8,128)S(1)} %get-tuple-element.7.ns_in), custom_call_target="tpu_custom_call" | custom-call | tf_op jit(solution)/shard_map/pallas_call | solution.py:655
